TPU v7x, 256 devices: a whole 4x4x8 slice. The times are simulated.
256 devices in a mesh: chan: 16 (over x_lo, z), bl: 16 (over y, x_hi, core).
Axes of the slice: x: 4 (x_hi: 2, x_lo: 2; x = x_hi * 2 + x_lo), y: 4, z: 8, core: 2. Of those that a mesh axis runs over, the one named last changes fastest.
Arguments:
- visibility: float32 [2, 2, 256, 8192], P(None, None, 'chan', 'bl'), may hold values from -12 to 12
- coherency: float32 [2, 2, 16, 256, 8192], P(None, None, None, 'chan', 'bl'), may hold values from -6 to 6
- station_pairs: int32 [2, 8192], P(None, 'bl'), may hold values from 0 to 511, as said below
- jones_gains: float32 [2, 2, 16, 256, 512], P(None, None, None, 'chan', 'bl'), may hold values from -1.2 to 2.2
- scaled_duals: float32 [2, 2, 16, 256, 512], P(None, None, None, 'chan', 'bl'), may hold values from -1.8 to 1.8
- penalty: float32 [16], replicated, may hold values from 5 to 50
Outputs:
- jones_out: float32 [2, 2, 16, 256, 512], P(None, None, None, 'chan', 'bl')
- duals_out: float32 [2, 2, 16, 256, 512], P(None, None, None, 'chan', 'bl')
Inputs may be any that keep to these rules, and one draw needn't show every extreme that they name: `station_pairs`: each row names two different stations.
All inputs are finite; a program needn't handle non-finite values.
Results may differ from a plain program's by a relative error of at most 0.00014.
Values sent between devices are 32-bit elements; how exact they have to be, the bound alone decides.
A program may use at most 128 MiB of HBM per device.

v0:
```python
import math

import jax
import jax.numpy as jnp
from jax import lax
from jax.sharding import PartitionSpec as P

STATION_COUNT = 512
FREQ_CHANNELS = 256
ITERS = 2
NPOLY = 3


def cosine_table(first_channel, channel_count):
    freq = (first_channel + lax.broadcasted_iota(jnp.int32, (channel_count, NPOLY), 0)).astype(
        jnp.float32
    )
    order = lax.broadcasted_iota(jnp.int32, (channel_count, NPOLY), 1).astype(jnp.float32)
    scale = jnp.where(order < 0.5, math.sqrt(1.0 / FREQ_CHANNELS), math.sqrt(2.0 / FREQ_CHANNELS))
    return scale * jnp.cos(math.pi * order * (freq + 0.5) / FREQ_CHANNELS)


def fit_terms(basis_table, target):
    return jnp.einsum("fb,rpkfs->rpkbs", basis_table, target, precision=lax.Precision.HIGHEST)


def spread_terms(basis_table, coeff):
    return jnp.einsum("fb,rpkbs->rpkfs", basis_table, coeff, precision=lax.Precision.HIGHEST)


def normal_terms(vis_data, coh_data, paired):
    row_count = vis_data.shape[-1]
    left_gain = paired[..., :row_count]
    right_gain = paired[..., row_count:]
    prod_re = left_gain[0] * coh_data[0] - left_gain[1] * coh_data[1]
    prod_im = left_gain[0] * coh_data[1] + left_gain[1] * coh_data[0]
    model_re = prod_re * right_gain[0] + prod_im * right_gain[1]
    model_im = prod_im * right_gain[0] - prod_re * right_gain[1]
    resid_re = (vis_data[0] - jnp.sum(model_re, axis=1))[:, None]
    resid_im = (vis_data[1] - jnp.sum(model_im, axis=1))[:, None]
    side_re = coh_data[0] * right_gain[0] + coh_data[1] * right_gain[1]
    side_im = coh_data[1] * right_gain[0] - coh_data[0] * right_gain[1]
    first_re = resid_re * side_re + resid_im * side_im
    first_im = resid_im * side_re - resid_re * side_im
    second_re = resid_re * prod_re + resid_im * prod_im
    second_im = resid_re * prod_im - resid_im * prod_re
    first_wt = side_re * side_re + side_im * side_im
    second_wt = prod_re * prod_re + prod_im * prod_im
    return jnp.stack(
        [
            jnp.concatenate([first_re, second_re], axis=-1),
            jnp.concatenate([first_im, second_im], axis=-1),
            jnp.concatenate([first_wt, second_wt], axis=-1),
        ]
    )


def advance(gain_state, dual_state, fitted, sums, penalty):
    weight = penalty[:, None, None]
    gain_state = gain_state + (sums[0:2] + weight * (fitted - dual_state - gain_state)) / (
        sums[2][None] + weight
    )
    dual_state = dual_state + gain_state - fitted
    return (gain_state, dual_state)


def body(visibility, coherency, station_pairs, jones_gains, scaled_duals, penalty):
    chan_count = jones_gains.shape[3]
    row_count = visibility.shape[3]
    basis_table = cosine_table(lax.axis_index("chan") * chan_count, chan_count)
    station_ids = jnp.concatenate([station_pairs[0], station_pairs[1]])
    stations = lax.broadcasted_iota(jnp.int32, (STATION_COUNT, 2 * row_count), 0)
    onehot = (stations == station_ids[None, :]).astype(jnp.float32)
    gain_state, dual_state = (jones_gains, scaled_duals)
    for iteration in range(ITERS):
        coeff = lax.psum(fit_terms(basis_table, gain_state + dual_state), "chan")
        fitted = spread_terms(basis_table, coeff)
        paired = lax.dot_general(
            lax.all_gather(gain_state, "bl", axis=4, tiled=True),
            onehot,
            (((4,), (0,)), ((), ())),
            precision=lax.Precision.HIGHEST,
            preferred_element_type=jnp.float32,
        )
        contrib = normal_terms(visibility, coherency, paired)
        owned = lax.psum_scatter(
            lax.dot_general(
                onehot,
                contrib,
                (((1,), (4,)), ((), ())),
                precision=lax.Precision.HIGHEST,
                preferred_element_type=jnp.float32,
            ),
            "bl",
            scatter_dimension=0,
            tiled=True,
        )
        sums = jnp.moveaxis(owned, 0, -1)
        gain_state, dual_state = advance(gain_state, dual_state, fitted, sums, penalty)
    return (gain_state, dual_state)


def solution(mesh):
    placed = (
        P(None, None, "chan", "bl"),
        P(None, None, None, "chan", "bl"),
        P(None, "bl"),
        P(None, None, None, "chan", "bl"),
        P(None, None, None, "chan", "bl"),
        P(),
    )
    return jax.shard_map(
        body,
        mesh=mesh,
        in_specs=placed,
        out_specs=(P(None, None, None, "chan", "bl"), P(None, None, None, "chan", "bl")),
        check_vma=False,
    )
```

profile of v0, /device:TPU:1, one launch (start us, length us, event | category | flops | bytes accessed | tf_op | source)
XLA Modules:
  0.0 496.7 jit_solution(17890262696159975860)
XLA Ops:
  7.2 2.8 copy.8
  10.1 119.2 %all-gather.3.cloned.1.call-done = f32[2,2,16,16,512]{3,2,1,0,4:T(8,128)} async-done(((f32[2,2,16,16,32]{3,2,1,0,4:T(8,128)}), f32[2,2,16,16,512]{3,2,1,0,4:T(8,128)}) %all-gather.3.cloned.1.call-update) | async-done | bytes 2097168 | tf_op jit(solution)/shard_map/all_gather | solution.py:79
  129.3 27.3 %fusion.16 = f32[2,2,16,16,1024]{4,3,2,1,0:T(8,128)S(1)} fusion(f32[2,2,16,16,512]{3,2,1,0,4:T(8,128)} %all-gather.3.cloned.1.call-done, s32[1024]{0:T(1024)S(1)} %pad_add_fusion), kind=kOutput, calls=%fused_computation.16 | convolution fusion | flops 6442975232 | bytes 6295552 | tf_op jit(solution)/shard_map/dot_general | solution.py:78
  156.6 0.8 add_reduce_fusion.1
  157.5 0.5 multiply_add_fusion.7
  158.0 1.0 multiply_add_fusion.6
  159.1 0.2 maximum_bitcast_fusion.2
  159.3 0.5 maximum_bitcast_fusion
  159.8 6.9 %fusion.4 = f32[512,3,2,16,16]{0,4,3,2,1:T(8,128)} fusion(f32[1,2,16,16,1024]{4,3,2,1,0:T(8,128)S(1)} %maximum_bitcast_fusion.2, f32[1,2,16,16,1024]{4,3,2,1,0:T(8,128)S(1)} %get-tuple-element.41, f32[1,2,16,16,1024]{4,3,2,1,0:T(8,128)S(1)} %get-tuple-element.40, s32[1024]{0:T(1024)S(1)} %pad_add_fusion), kind=kOutput, calls=%fused_computation.4 | convolution fusion | flops 9667346432 | bytes 9441280 | tf_op jit(solution)/shard_map/dot_general | solution.py:87
  166.7 3.5 copy.18
  170.3 0.9 copy-done.1
  171.4 0.5 convolution_bitcast_fusion.3
  171.9 51.3 %psum.14 = f32[2,2,16,3,32]{4,3,2,1,0:T(4,128)} all-reduce(f32[2,2,16,3,32]{4,3,2,1,0:T(4,128)S(1)} %convolution_bitcast_fusion.3), channel_id=1, replica_groups=mesh['chan'=16,'bl'=16] {'chan'}, use_global_device_ids=true, to_apply=%region_3.4 | all-reduce | flops 6144 | bytes 49152 | tf_op jit(solution)/shard_map/psum | solution.py:76
  223.2 26.4 %reduce-scatter.7.cloned.1.call-done = f32[32,1536]{1,0:T(8,128)} async-done(((f32[512,1536]{1,0:T(8,128)}), f32[32,1536]{1,0:T(8,128)}) %reduce-scatter.7.cloned.1.call-update) | async-done | bytes 196624
  249.6 1.2 copy.19
  250.8 0.9 copy-done.4
  251.6 0.7 fusion.43
  252.4 2.9 fusion.39
  255.3 1.7 copy.10
  257.1 114.9 %all-gather.5.cloned.1.call-done = f32[2,2,16,16,512]{3,2,1,0,4:T(8,128)} async-done(((f32[2,2,16,16,32]{3,2,1,0,4:T(8,128)}), f32[2,2,16,16,512]{3,2,1,0,4:T(8,128)}) %all-gather.5.cloned.1.call-update) | async-done | bytes 2097168 | tf_op jit(solution)/shard_map/all_gather | solution.py:79
  371.9 22.5 %fusion = f32[2,2,16,16,1024]{4,3,2,1,0:T(8,128)S(1)} fusion(f32[2,2,16,16,512]{3,2,1,0,4:T(8,128)} %all-gather.5.cloned.1.call-done, s32[1024]{0:T(1024)S(1)} %pad_add_fusion), kind=kOutput, calls=%fused_computation | convolution fusion | flops 6442975232 | bytes 6295552 | tf_op jit(solution)/shard_map/dot_general | solution.py:78
  394.4 0.8 add_reduce_fusion
  395.2 0.6 multiply_add_fusion.3
  395.8 0.9 multiply_add_fusion.2
  397.2 6.9 %fusion.10 = f32[512,3,2,16,16]{0,4,3,2,1:T(8,128)} fusion(f32[1,2,16,16,1024]{4,3,2,1,0:T(8,128)S(1)} %maximum_bitcast_fusion.5, f32[1,2,16,16,1024]{4,3,2,1,0:T(8,128)S(1)} %maximum_bitcast_fusion.4, f32[1,2,16,16,1024]{4,3,2,1,0:T(8,128)S(1)} %maximum_bitcast_fusion.3, s32[1024]{0:T(1024)S(1)} %pad_add_fusion), kind=kOutput, calls=%fused_computation.10 | convolution fusion | flops 9667346432 | bytes 9441280 | tf_op jit(solution)/shard_map/dot_general | solution.py:87
  404.1 3.5 copy.20
  407.7 1.0 copy-done.3
  408.7 0.5 convolution_bitcast_fusion.2
  409.2 50.7 %psum.15 = f32[2,2,16,3,32]{4,3,2,1,0:T(4,128)S(1)} all-reduce(f32[2,2,16,3,32]{4,3,2,1,0:T(4,128)S(1)} %convolution_bitcast_fusion.2), channel_id=1, replica_groups=mesh['chan'=16,'bl'=16] {'chan'}, use_global_device_ids=true, to_apply=%region_7.8 | all-reduce | flops 6144 | bytes 49152 | tf_op jit(solution)/shard_map/psum | solution.py:76
  459.9 27.2 %reduce-scatter.9.cloned.1.call-done = f32[32,1536]{1,0:T(8,128)} async-done(((f32[512,1536]{1,0:T(8,128)}), f32[32,1536]{1,0:T(8,128)}) %reduce-scatter.9.cloned.1.call-update) | async-done | bytes 196624
  487.0 1.2 copy.21
  488.3 1.9 add_subtract_fusion
  (31 shorter events, 1.2 us)
Async XLA Ops:
  7.2 2.9 copy-start.7
  7.2 122.1 %all-gather.3.cloned.1.call-start = ((), (), s32[]{:S(2)}) async-start(), calls=%async_computation.2 | async-start | bytes 17825792 | tf_op jit(solution)/shard_map/all_gather | solution.py:79
  10.0 239.5 %reduce-scatter.7.cloned.1.call-start = ((), (), s32[]{:S(2)}) async-start(), calls=%async_computation.4 | async-start | bytes 3342336
  10.1 146.4 %copy-start = (f32[2,2,16,16,512]{4,3,2,1,0:T(8,128)S(1)}, f32[2,2,16,16,512]{4,3,2,1,0:T(8,128)}, u32[]{:S(2)}) copy-start(f32[2,2,16,16,512]{4,3,2,1,0:T(8,128)} %param.7) | copy-start | bytes 6291460
  156.6 0.9 copy-start.5
  170.2 1.0 copy-start.1
  170.2 1.2 copy-start.2
  170.2 201.7 %all-gather.5.cloned.1.call-start = ((), (), s32[]{:S(2)}) async-start(), calls=%async_computation.3 | async-start | bytes 17825792 | tf_op jit(solution)/shard_map/all_gather | solution.py:79
  250.8 0.9 copy-start.4
  257.0 230.0 %reduce-scatter.9.cloned.1.call-start = ((), (), s32[]{:S(2)}) async-start(), calls=%async_computation.5 | async-start | bytes 3342336
  407.6 1.0 copy-start.3
  407.7 80.6 %copy-start.6 = (f32[16]{0:T(128)S(1)}, f32[16]{0:T(128)}, u32[]{:S(2)}) copy-start(f32[16]{0:T(128)} %param.11) | copy-start | bytes 196
Sparse Core Ops, SparseCore 0:
  10.8 118.4 all-gather.2
  170.3 79.1 reduce-scatter.6
  257.1 114.7 all-gather.4
  407.8 79.1 reduce-scatter.8
where the time goes:
time: 497 us
  waiting for transfers between devices  288 us (58%)
  blocking collectives  102 us (21%)
  matrix products  69.2 us (14%)
  local copies, waits for them, and re-layouts  17 us (3%)
  between operations  14 us (3%)
  other arithmetic  6.75 us (1%)
    all_gather x2, waiting for transfers between devices, body(): lax.all_gather(gain_state, 'bl', axis=4, tiled=True)  234 us
    psum x2, blocking collectives, body(): coeff = lax.psum(fit_terms(basis_table, gain_state + dual_state), 'chan')  102 us
    unnamed x6, waiting for transfers between devices  53.6 us
    dot_general x2, matrix products, body(): lax.dot_general(lax.all_gather(gain_state, 'bl', axis=4, tiled=True), one...  49.7 us
    unnamed x21, local copies, waits for them, and re-layouts  15.3 us
    dot_general x2, matrix products, body(): lax.dot_general(onehot, contrib, (((1,), (4,)), ((), ())), precision=lax....  13.7 us
  transfers between devices with their start and end apart: 4, of which 4 were waited for; matrix products, arithmetic and copies ran while one was open for 0% of the time, Pallas kernels for 0%

commit v1 on v0

v1 whole, which is shorter than its diff:
```python
import functools
import math

import jax
import jax.numpy as jnp
import numpy as np
from jax import lax
from jax.experimental import pallas as pl
from jax.experimental.pallas import tpu as pltpu
from jax.sharding import PartitionSpec as P

STATIONS = 512
CHANNELS = 256
NPOLY = 3
DIRS = 16
GROUP = 16
ROWS = 512
OWN = STATIONS // GROUP
HALF = 256
MESH = pl.DeviceIdType.MESH
f32, bf16 = jnp.float32, jnp.bfloat16


def cosine_table():
    freq = np.arange(CHANNELS, dtype=np.float64)[:, None]
    order = np.arange(NPOLY, dtype=np.float64)[None, :]
    scale = np.where(order < 0.5, math.sqrt(1.0 / CHANNELS), math.sqrt(2.0 / CHANNELS))
    return (scale * np.cos(math.pi * order * (freq + 0.5) / CHANNELS)).astype(np.float32)


def split(x):
    hi = x.astype(bf16)
    return hi, (x - hi.astype(f32)).astype(bf16)


def regroup(blocks):
    lane = lax.broadcasted_iota(jnp.int32, blocks[0].shape, 1) // OWN
    outs = []
    for i in range(4):
        out = None
        for a, block in enumerate(blocks):
            shift = (OWN * (a - i)) % 128
            moved = pltpu.roll(block, shift, 1) if shift else block
            out = moved if out is None else jnp.where(lane == a, moved, out)
        outs.append(out)
    return outs


def build_onehot(c_ref, oh_ref, b):
    station = lax.broadcasted_iota(jnp.int32, (HALF, ROWS), 0).astype(f32)
    for side in range(2):
        pair = c_ref[b, 68 + side : 69 + side, :]
        low = jnp.where(pair >= HALF, pair - HALF, pair)
        oh_ref[b, :, side * ROWS : (side + 1) * ROWS] = jnp.where(station == low, 1.0, 0.0).astype(bf16)


def set_table(g_ref, gcat_ref):
    for row in range(0, 64, 16):
        for half in range(2):
            hi, lo = split(g_ref[row : row + 16, half * HALF : (half + 1) * HALF])
            gcat_ref[half * 128 + row : half * 128 + row + 16, :] = hi
            gcat_ref[half * 128 + 64 + row : half * 128 + 80 + row, :] = lo


def row_terms(c_ref, x_ref, s_ref, b, n=128):
    for l in range(0, ROWS, n):
        upper = [
            jnp.broadcast_to(c_ref[b, 68 + side : 69 + side, l : l + n] >= HALF, (DIRS, n))
            for side in range(2)
        ]
        for pol in range(2):

            def gain(side, part):
                o = part * 32 + pol * 16
                at = slice(side * ROWS + l, side * ROWS + l + n)
                h0, l0, h1, l1 = [x_ref[k + o : k + o + 16, at] for k in (0, 64, 128, 192)]
                return jnp.where(upper[side], h1, h0) + jnp.where(upper[side], l1, l0)

            pr, pi, qr, qi = gain(0, 0), gain(0, 1), gain(1, 0), gain(1, 1)
            cr = c_ref[b, 16 * pol : 16 * pol + 16, l : l + n]
            ci = c_ref[b, 32 + 16 * pol : 48 + 16 * pol, l : l + n]
            dr = pr * cr - pi * ci
            di = pr * ci + pi * cr
            mr = dr * qr + di * qi
            mi = di * qr - dr * qi
            rr = c_ref[b, 64 + pol : 65 + pol, l : l + n] - jnp.sum(mr, axis=0, keepdims=True)
            ri = c_ref[b, 66 + pol : 67 + pol, l : l + n] - jnp.sum(mi, axis=0, keepdims=True)
            sr = cr * qr + ci * qi
            si = ci * qr - cr * qi
            first = (rr * sr + ri * si, ri * sr - rr * si, sr * sr + si * si)
            second = (rr * dr + ri * di, rr * di - ri * dr, dr * dr + di * di)
            for side, terms in enumerate((first, second)):
                for comp, term in enumerate(terms):
                    for half in range(2):
                        if half:
                            kept = jnp.where(upper[side], term, 0.0)
                        else:
                            kept = jnp.where(upper[side], 0.0, term)
                        hi, lo = split(kept)
                        o = half * 192 + comp * 32 + pol * 16
                        at = slice(side * ROWS + l, side * ROWS + l + n)
                        s_ref[o : o + 16, at] = hi
                        s_ref[o + 96 : o + 112, at] = lo


def kernel(
    coh, vis, pairs, jones, duals, pen, table,
    jones_out, duals_out,
    raw, vraw, cown, C, J, U, J1, S2, g_ref, u_own, usend, j1send, s2send, coef, xbuf, zbuf,
    oh, gcat, x_ref, s_ref, acc,
    ssem, rsem, lsem, cs, cr,
):
    ch = lax.axis_index("chan")
    me = lax.axis_index("bl")
    y, x, c = me // 4, (me // 2) % 2, me % 2
    xl, z = ch // 8, ch % 8

    def to(o):
        return ((y + o // 4) % 4) * 4 + ((x + (o // 2) % 2) % 2) * 2 + (c + o % 2) % 2

    def fro(o):
        return ((y + 4 - o // 4) % 4) * 4 + ((x + (o // 2) % 2) % 2) * 2 + (c + o % 2) % 2

    def xpeer():
        return {"chan": (1 - xl) * 8 + z}

    def zpeer(o):
        return {"chan": xl * 8 + (z + o) % 8}

    barrier = pltpu.get_barrier_semaphore()

    @pl.loop(1, GROUP)
    def _(o):
        pl.semaphore_signal(barrier, inc=1, device_id={"bl": to(o)}, device_id_type=MESH)

    pl.semaphore_signal(barrier, inc=1, device_id=xpeer(), device_id_type=MESH)

    @pl.loop(1, 8)
    def _(o):
        pl.semaphore_signal(barrier, inc=1, device_id=zpeer(o), device_id_type=MESH)

    mine = [
        pltpu.make_async_copy(
            src.at[:, pl.ds(128 * t, 128)], dst.at[pl.ds(t * deep, deep)], lsem.at[i, t]
        )
        for t in range(ROWS // 128)
        for i, (src, dst, deep) in enumerate(((coh, raw, 64 * GROUP), (vis, vraw, 4 * GROUP)))
    ]
    for copy in mine:
        copy.start()
    J[me] = jones[me]
    fill = jnp.concatenate([pairs[...].astype(f32), jnp.zeros((2, ROWS), f32)], axis=0)
    for copy in mine:
        copy.wait()

    @pl.loop(0, GROUP)
    def _(f):
        for t in range(ROWS // 128):
            at = slice(128 * t, 128 * t + 128)
            for k in range(0, 64, 8):
                cown[f, k : k + 8, at] = raw[pl.ds(f + (64 * t + k) * GROUP, 8, stride=GROUP)]
            cown[f, 64:68, at] = vraw[pl.ds(f + 4 * t * GROUP, 4, stride=GROUP)]
        cown[f, 68:72] = fill

    C[me] = cown[me]
    pl.semaphore_wait(barrier, 23)

    def remote(kind, o, src, dst):
        return pltpu.make_async_remote_copy(
            src_ref=src, dst_ref=dst, send_sem=ssem.at[kind, o], recv_sem=rsem.at[kind, o],
            device_id={"bl": to(o)}, device_id_type=MESH,
        )

    def jones_to(o):
        return remote(0, o, jones.at[to(o)], J.at[me])

    def coh_to(o):
        return remote(1, o, cown.at[to(o)], C.at[me])

    def u_to(o):
        return remote(2, o, usend.at[to(o)], U.at[me])

    def j1_to(o):
        return remote(3, o, j1send.at[to(o)], J1.at[me])

    def s2_to(o):
        return remote(4, o, s2send.at[to(o)], S2.at[me])

    def x_copy(it):
        return pltpu.make_async_remote_copy(
            src_ref=coef.at[2 * it], dst_ref=xbuf.at[it], send_sem=cs.at[it, 0], recv_sem=cr.at[it, 0],
            device_id=xpeer(), device_id_type=MESH,
        )

    def z_copy(it, o):
        return pltpu.make_async_remote_copy(
            src_ref=coef.at[2 * it + 1], dst_ref=zbuf.at[it, o], send_sem=cs.at[it, o], recv_sem=cr.at[it, o],
            device_id=zpeer(o), device_id_type=MESH,
        )

    @pl.loop(1, GROUP)
    def _(o):
        jones_to(o).start()

    @pl.loop(1, GROUP)
    def _(o):
        coh_to(o).start()

    def basis(f, b):
        return table[(ch * GROUP + f) * NPOLY + b]

    def fit(it, target):
        total = [jnp.zeros((DIRS, 128), f32) for _ in range(NPOLY)]
        for f in range(GROUP):
            value = target(f)
            for b in range(NPOLY):
                total[b] += basis(f, b) * value
        for b in range(NPOLY):
            coef[2 * it, b] = total[b]
        x_copy(it).start()

    def fit_x(it):
        x_copy(it).wait_recv()
        coef[2 * it + 1] = coef[2 * it] + xbuf[it]

        @pl.loop(1, 8)
        def _(o):
            z_copy(it, o).start()

    def fit_z(it):
        @pl.loop(1, 8)
        def _(o):
            z_copy(it, o).wait_recv()

        total = [coef[2 * it + 1, b] for b in range(NPOLY)]
        for o in range(1, 8):
            for b in range(NPOLY):
                total[b] += zbuf[it, o, b]

        def fitted(f):
            return sum(basis(f, b) * total[b] for b in range(NPOLY))

        return fitted

    fit(0, lambda f: jones[f] + duals[f])
    fit_x(0)
    fitted = fit_z(0)
    for f in range(GROUP):
        u_own[f] = fitted(f) - duals[f]
    usend[...] = u_own[...]
    U[me] = u_own[me]

    @pl.loop(1, GROUP)
    def _(o):
        u_to(o).start()


    @pl.loop(1, GROUP)
    def _(o):
        jones_to(o).wait_recv()

    for q in range(4):
        for a, block in enumerate(regroup([J[4 * q + i] for i in range(4)])):
            g_ref[16 * a : 16 * a + 16, 128 * q : 128 * q + 128] = block
    set_table(g_ref, gcat)
    acc[...] = jnp.zeros_like(acc)

    def block(b):
        x_ref[...] = jnp.dot(gcat[...], oh[b], preferred_element_type=f32)
        row_terms(C, x_ref, s_ref, b)
        acc[...] += lax.dot_general(
            s_ref[...], oh[b], (((1,), (1,)), ((), ())), preferred_element_type=f32
        )

    @pl.loop(0, GROUP)
    def _(o):
        b = fro(o)

        @pl.when(o > 0)
        def _():
            coh_to(o).wait_recv()

        build_onehot(C, oh, b)
        block(b)

    def sums(comp, pol, q):
        o, at = (q // 2) * 192 + comp * 32 + pol * 16, slice((q % 2) * 128, (q % 2) * 128 + 128)
        return acc[o : o + 16, at] + acc[o + 96 : o + 112, at]

    row = lax.broadcasted_iota(jnp.int32, (DIRS, 128), 0)
    weight = jnp.zeros((DIRS, 128), f32)
    for k in range(DIRS):
        weight = jnp.where(row == k, pen[k], weight)

    @pl.loop(1, GROUP)
    def _(o):
        u_to(o).wait_recv()

    for q in range(4):
        u = regroup([U[4 * q + i] for i in range(4)])
        wide = [sums(2, pol, q) + weight for pol in range(2)]
        new = []
        for a in range(4):
            gain = g_ref[16 * a : 16 * a + 16, 128 * q : 128 * q + 128]
            gain = gain + (sums(a // 2, a % 2, q) + weight * (u[a] - gain)) / wide[a % 2]
            g_ref[16 * a : 16 * a + 16, 128 * q : 128 * q + 128] = gain
            new.append(gain)
        for i, slab in enumerate(regroup(new)):
            j1send[4 * q + i] = slab
    J1[me] = j1send[me]

    @pl.loop(1, GROUP)
    def _(o):
        j1_to(o).start()

    set_table(g_ref, gcat)
    acc[...] = jnp.zeros_like(acc)

    @pl.loop(0, 4)
    def _(o):
        block(o)

    @pl.loop(1, GROUP)
    def _(o):
        j1_to(o).wait_recv()

    fit(1, lambda f: 2.0 * J1[f] - u_own[f])

    @pl.loop(4, 8)
    def _(o):
        block(o)

    fit_x(1)

    @pl.loop(8, 14)
    def _(o):
        block(o)

    fitted = fit_z(1)
    for f in range(GROUP):
        u_own[f] = fitted(f) - (J1[f] - u_own[f])

    @pl.loop(14, 16)
    def _(o):
        block(o)

    for q in range(4):
        grads = regroup([sums(a // 2, a % 2, q) for a in range(4)])
        wides = [sums(2, pol, q) for pol in range(2)]
        wides = regroup([wides[a % 2][8 * (a // 2) : 8 * (a // 2) + 8] for a in range(4)])
        for i in range(4):
            s2send[4 * q + i, 0:16] = grads[i]
            s2send[4 * q + i, 16:24] = wides[i]
    S2[me] = s2send[me]

    @pl.loop(1, GROUP)
    def _(o):
        s2_to(o).start()

    @pl.loop(1, GROUP)
    def _(o):
        s2_to(o).wait_recv()

    low = lax.broadcasted_iota(jnp.int32, (8, 128), 1) < 64
    for f in range(GROUP):
        packed = S2[f, 16:24]
        turned = pltpu.roll(packed, 64, 1)
        for h, wide in enumerate((jnp.where(low, packed, turned), jnp.where(low, turned, packed))):
            at = slice(8 * h, 8 * h + 8)
            gain, u, pk = J1[f, at], u_own[f, at], weight[at]
            gain = gain + (S2[f, at] + pk * (u - gain)) / (wide + pk)
            jones_out[f, at] = gain
            duals_out[f, at] = gain - u

    @pl.loop(1, GROUP)
    def _(o):
        for copy in (jones_to, coh_to, u_to, j1_to, s2_to):
            copy(o).wait_send()

    for it in range(2):
        x_copy(it).wait_send()

        @pl.loop(1, 8)
        def _(o):
            z_copy(it, o).wait_send()


def body(visibility, coherency, station_pairs, jones_gains, scaled_duals, penalty):
    def pack(state):
        return jnp.transpose(state, (3, 2, 0, 1, 4)).reshape(GROUP, DIRS, 128)

    def unpack(state):
        return jnp.transpose(state.reshape(GROUP, DIRS, 2, 2, OWN), (2, 3, 1, 0, 4))

    slab = (GROUP, DIRS, 128)
    out = jax.ShapeDtypeStruct(slab, f32)
    hbm, vmem, smem = [
        pl.BlockSpec(memory_space=space) for space in (pltpu.HBM, pltpu.VMEM, pltpu.SMEM)
    ]
    jones, duals = pl.pallas_call(
        kernel,
        out_shape=(out, out),
        in_specs=[hbm, hbm, vmem, vmem, vmem, smem, smem],
        out_specs=(vmem, vmem),
        scratch_shapes=[
            pltpu.VMEM((4 * 64 * GROUP, 128), f32),
            pltpu.VMEM((4 * 4 * GROUP, 128), f32),
            pltpu.VMEM((GROUP, 72, ROWS), f32),
            pltpu.VMEM((GROUP, 72, ROWS), f32),
            pltpu.VMEM(slab, f32),
            pltpu.VMEM(slab, f32),
            pltpu.VMEM(slab, f32),
            pltpu.VMEM((GROUP, 24, 128), f32),
            pltpu.VMEM((64, STATIONS), f32),
            pltpu.VMEM(slab, f32),
            pltpu.VMEM(slab, f32),
            pltpu.VMEM(slab, f32),
            pltpu.VMEM((GROUP, 24, 128), f32),
            pltpu.VMEM((4, NPOLY, DIRS, 128), f32),
            pltpu.VMEM((2, NPOLY, DIRS, 128), f32),
            pltpu.VMEM((2, 8, NPOLY, DIRS, 128), f32),
            pltpu.VMEM((GROUP, HALF, 2 * ROWS), bf16),
            pltpu.VMEM((256, HALF), bf16),
            pltpu.VMEM((256, 2 * ROWS), f32),
            pltpu.VMEM((384, 2 * ROWS), bf16),
            pltpu.VMEM((384, HALF), f32),
            pltpu.SemaphoreType.DMA((5, GROUP)),
            pltpu.SemaphoreType.DMA((5, GROUP)),
            pltpu.SemaphoreType.DMA((2, 4)),
            pltpu.SemaphoreType.DMA((2, 8)),
            pltpu.SemaphoreType.DMA((2, 8)),
        ],
        compiler_params=pltpu.CompilerParams(
            collective_id=0, has_side_effects=True, vmem_limit_bytes=48 * 2**20
        ),
    )(
        coherency.reshape(64 * GROUP, ROWS),
        visibility.reshape(4 * GROUP, ROWS),
        station_pairs,
        pack(jones_gains),
        pack(scaled_duals),
        penalty,
        jnp.asarray(cosine_table().reshape(-1)),
    )
    return unpack(jones), unpack(duals)


def solution(mesh):
    state = P(None, None, None, "chan", "bl")
    return jax.shard_map(
        body,
        mesh=mesh,
        in_specs=(P(None, None, "chan", "bl"), state, P(None, "bl"), state, state, P()),
        out_specs=(state, state),
        check_vma=False,
    )
```

time: 497 us -> 94.2 us (0.19)
  waiting for transfers between devices: 288 us -> 0 us
  blocking collectives: 102 us -> 0 us
  Pallas kernels: 0 us -> 87 us
  matrix products: 69.2 us -> 0 us
  between operations: 14 us -> 0.72 us
  local copies, waits for them, and re-layouts: 17 us -> 6.41 us
  other arithmetic: 6.75 us -> 0 us
    all_gather x2 -> x0, waiting for transfers between devices: 234 us -> none  [body(): lax.all_gather(gain_state, 'bl', axis=4, tiled=True)]
    psum x2 -> x0, blocking collectives: 102 us -> none  [body(): coeff = lax.psum(fit_terms(basis_table, gain_state + dual_state), 'chan')]
    pallas_call x0 -> x1, Pallas kernels: none -> 87 us  [body(): pl.pallas_call(kernel, out_shape=(out, out), in_specs=[hbm, hbm, vmem, vm...]
    dot_general x8 -> x0, matrix products: 69.2 us -> none  [the longest x2 49.7 us: body(): lax.dot_general(lax.all_gather(gain_state, 'bl', axis=4, tiled=True), one...]
    unnamed x6 -> x0, waiting for transfers between devices: 53.6 us -> none
    unnamed x21 -> x10, local copies, waits for them, and re-layouts: 15.3 us -> 0.02 us
  transfers between devices with their start and end apart: 4 -> 0, of which waited for: 4 -> 0; matrix products, arithmetic and copies ran while one was open for 0% -> 0% of each run, Pallas kernels for 0% -> 0%
where the time goes in v1:
time: 94.2 us; the launch traced here: 94.1 us
  Pallas kernels  87 us (92%)
  local copies, waits for them, and re-layouts  6.41 us (7%)
    pallas_call x1, Pallas kernels, body(): pl.pallas_call(kernel, out_shape=(out, out), in_specs=[hbm, hbm, vmem, vm...  87 us
    transpose x2, local copies, waits for them, and re-layouts, pack(): return jnp.transpose(state, (3, 2, 0, 1, 4)).reshape(GROUP, DIRS, 128)  3.05 us

profile of v1, /device:TPU:1, one launch (start us, length us, event | category | flops | bytes accessed | tf_op | source)
XLA Modules:
  0.0 94.1 jit_solution(13327574279073940247)
XLA Ops:
  0.6 0.0 copy-start.3
  0.6 0.0 copy-start.4
  0.7 0.0 copy-start.2
  0.7 0.0 copy-start
  0.7 0.0 copy-start.1
  0.7 1.6 %copy.9 = f32[16,16,2,2,32]{4,3,2,1,0:T(2,128)S(1)} copy(f32[16,16,2,2,32]{4,0,1,3,2:T(8,128)} %bitcast.10) | data formatting | bytes 262144 | tf_op jit(solution)/shard_map/transpose | solution.py:390
  2.3 0.4 reshape.24.jones
  2.7 1.5 %copy.10 = f32[16,16,2,2,32]{4,3,2,1,0:T(2,128)S(1)} copy(f32[16,16,2,2,32]{4,0,1,3,2:T(8,128)} %bitcast.11) | data formatting | bytes 262144 | tf_op jit(solution)/shard_map/transpose | solution.py:390
  4.2 0.4 reshape.25.duals
  4.6 0.0 copy-done.3
  4.6 0.0 copy-done.4
  4.6 0.0 copy-done.2
  4.6 0.0 copy-done
  4.7 0.0 copy-done.1
  4.7 87.0 %shard_map.86 = (f32[16,16,128]{2,1,0:T(8,128)S(1)}, f32[16,16,128]{2,1,0:T(8,128)S(1)}) custom-call(f32[1024,512]{1,0:T(8,128)S(1)} %bitcast.8, f32[64,512]{1,0:T(8,128)S(1)} %bitcast.9, s32[2,512]{1,0:T(2,128)S(1)} %copy-done.2, f32[16,16,128]{2,1,0:T(8,128)S(1)} %reshape.24.jones, f32[16,16,128]{2,1,0:T(8,128)S(1)} %reshape.25.duals, f32[16]{0:T(128)S(1)} %copy-done.4, ...), custom_call_target="tpu_custom_call" | custom-call | tf_op jit(solution)/shard_map/pallas_call | solution.py:400
  91.6 0.4 reshape.26
  92.1 0.4 reshape.27
  92.5 1.6 %copy_bitcast_fusion = (f32[2,2,16,16,32]{4,3,2,1,0:T(8,128)}, f32[2,2,16,16,32]{4,3,2,1,0:T(8,128)}) fusion(f32[16,16,2,2,32]{4,3,2,1,0:T(2,128)S(1)} %reshape.27, f32[16,16,2,2,32]{4,3,2,1,0:T(2,128)S(1)} %reshape.26), kind=kLoop, calls=%fused_computation | loop fusion | bytes 524288 | tf_op jit(solution)/shard_map/transpose | solution.py:393
Async XLA Ops:
  0.6 4.0 %copy-start.3 = (f32[768]{0:T(1024)S(1)}, f32[768]{0:T(1024)}, u32[]{:S(2)}) copy-start(f32[768]{0:T(1024)} %constant.2.clone.table) | copy-start | bytes 9220
  0.6 4.0 %copy-start.4 = (f32[16]{0:T(128)S(1)}, f32[16]{0:T(128)}, u32[]{:S(2)}) copy-start(f32[16]{0:T(128)} %pen.1) | copy-start | bytes 196
  0.7 4.0 %copy-start.2 = (s32[2,512]{1,0:T(2,128)S(1)}, s32[2,512]{1,0:T(2,128)}, u32[]{:S(2)}) copy-start(s32[2,512]{1,0:T(2,128)} %pairs.1) | copy-start | bytes 12292
  0.7 4.0 %copy-start = (f32[2,2,16,16,512]{4,3,2,1,0:T(8,128)S(1)}, f32[2,2,16,16,512]{4,3,2,1,0:T(8,128)}, u32[]{:S(2)}) copy-start(f32[2,2,16,16,512]{4,3,2,1,0:T(8,128)} %param.8) | copy-start | bytes 6291460
  0.7 4.0 %copy-start.1 = (f32[2,2,16,512]{3,2,1,0:T(8,128)S(1)}, f32[2,2,16,512]{3,2,1,0:T(8,128)}, u32[]{:S(2)}) copy-start(f32[2,2,16,512]{3,2,1,0:T(8,128)} %param.7) | copy-start | bytes 393220

commit v2 on v1

v2 whole, which is shorter than its diff:
```python
import functools
import math

import jax
import jax.numpy as jnp
import numpy as np
from jax import lax
from jax.experimental import pallas as pl
from jax.experimental.pallas import tpu as pltpu
from jax.sharding import PartitionSpec as P

STATIONS = 512
CHANNELS = 256
NPOLY = 3
DIRS = 16
GROUP = 16
ROWS = 512
OWN = STATIONS // GROUP
HALF = 256
LOGICAL = pl.DeviceIdType.LOGICAL
ZORDER = (1, 7, 2, 6, 3, 5, 4)
f32, bf16 = jnp.float32, jnp.bfloat16


def cosine_table():
    freq = np.arange(CHANNELS, dtype=np.float64)[:, None]
    order = np.arange(NPOLY, dtype=np.float64)[None, :]
    scale = np.where(order < 0.5, math.sqrt(1.0 / CHANNELS), math.sqrt(2.0 / CHANNELS))
    return (scale * np.cos(math.pi * order * (freq + 0.5) / CHANNELS)).astype(np.float32)


def split(x):
    hi = x.astype(bf16)
    return hi, (x - hi.astype(f32)).astype(bf16)


def regroup(blocks):
    lane = lax.broadcasted_iota(jnp.int32, blocks[0].shape, 1) // OWN
    outs = []
    for i in range(4):
        out = None
        for a, block in enumerate(blocks):
            shift = (OWN * (a - i)) % 128
            moved = pltpu.roll(block, shift, 1) if shift else block
            out = moved if out is None else jnp.where(lane == a, moved, out)
        outs.append(out)
    return outs


def build_onehot(j_ref, oh_ref, b):
    station = lax.broadcasted_iota(jnp.int32, (HALF, 128), 0).astype(f32)
    for k in range(8):
        pair = j_ref[b, DIRS + k : DIRS + k + 1, :]
        low = jnp.where(pair >= HALF, pair - HALF, pair)
        oh_ref[b, :, 128 * k : 128 * k + 128] = jnp.where(station == low, 1.0, 0.0).astype(bf16)


def set_table(g_ref, gcat_ref):
    for row in range(0, 64, 16):
        for half in range(2):
            hi, lo = split(g_ref[row : row + 16, half * HALF : (half + 1) * HALF])
            gcat_ref[half * 128 + row : half * 128 + row + 16, :] = hi
            gcat_ref[half * 128 + 64 + row : half * 128 + 80 + row, :] = lo


def row_terms(c_ref, j_ref, x_ref, s_ref, b, n=128):
    for l in range(0, ROWS, n):
        upper = [
            jnp.broadcast_to(j_ref[b, pl.ds(DIRS + 4 * side + l // n, 1), :] >= HALF, (DIRS, n))
            for side in range(2)
        ]
        for pol in range(2):

            def gain(side, part):
                o = part * 32 + pol * 16
                at = slice(side * ROWS + l, side * ROWS + l + n)
                h0, l0, h1, l1 = [x_ref[k + o : k + o + 16, at] for k in (0, 64, 128, 192)]
                return jnp.where(upper[side], h1, h0) + jnp.where(upper[side], l1, l0)

            pr, pi, qr, qi = gain(0, 0), gain(0, 1), gain(1, 0), gain(1, 1)
            cr = c_ref[b, 16 * pol : 16 * pol + 16, l : l + n]
            ci = c_ref[b, 32 + 16 * pol : 48 + 16 * pol, l : l + n]
            dr = pr * cr - pi * ci
            di = pr * ci + pi * cr
            mr = dr * qr + di * qi
            mi = di * qr - dr * qi
            rr = c_ref[b, 64 + pol : 65 + pol, l : l + n] - jnp.sum(mr, axis=0, keepdims=True)
            ri = c_ref[b, 66 + pol : 67 + pol, l : l + n] - jnp.sum(mi, axis=0, keepdims=True)
            sr = cr * qr + ci * qi
            si = ci * qr - cr * qi
            first = (rr * sr + ri * si, ri * sr - rr * si, sr * sr + si * si)
            second = (rr * dr + ri * di, rr * di - ri * dr, dr * dr + di * di)
            for side, terms in enumerate((first, second)):
                for comp, term in enumerate(terms):
                    for half in range(2):
                        if half:
                            kept = jnp.where(upper[side], term, 0.0)
                        else:
                            kept = jnp.where(upper[side], 0.0, term)
                        hi, lo = split(kept)
                        o = half * 192 + comp * 32 + pol * 16
                        at = slice(side * ROWS + l, side * ROWS + l + n)
                        s_ref[o : o + 16, at] = hi
                        s_ref[o + 96 : o + 112, at] = lo


def wrap(v, n):
    return jnp.where(v >= n, v - n, v)


def kernel(
    coh, vis, pairs, jones, duals, pen, table,
    jones_out, duals_out,
    raw, vraw, jraw, draw, jwide, dwide, cown, jmsg, dual, C, J, U, J1, S2, g_ref, u_own, usend, j1send, s2send,
    coef, xbuf, zbuf, oh, gcat, acc, x0, x1, x2, x3, s0, s1, s2, s3,
    ssem, rsem, lsem, cs, cr,
):
    ch = lax.axis_index("chan")
    me = lax.axis_index("bl")
    y, x, c = me // 4, (me // 2) % 2, me % 2
    xl, z = ch // 8, ch % 8
    base = ch * GROUP
    ys = [y] + [wrap(y + d, 4) for d in (1, 2, 3)]
    to = [ys[o // 4] * 4 + (x, 1 - x)[(o // 2) % 2] * 2 + (c, 1 - c)[o % 2] for o in range(GROUP)]
    xpeer = ((1 - xl) * 8 + z) * GROUP + me
    zpeer = [(xl * 8 + wrap(z + o, 8)) * GROUP + me for o in range(8)]

    def fro(o):
        return wrap(y + 4 - o // 4, 4) * 4 + wrap(x + (o // 2) % 2, 2) * 2 + wrap(c + o % 2, 2)

    mine = [
        pltpu.make_async_copy(jones, jraw, lsem.at[2, 0]),
        pltpu.make_async_copy(duals, draw, lsem.at[2, 1]),
    ] + [
        pltpu.make_async_copy(
            src.at[:, pl.ds(128 * t, 128)], dst.at[pl.ds(t * deep, deep)], lsem.at[i, t]
        )
        for t in range(ROWS // 128)
        for i, (src, dst, deep) in enumerate(((coh, raw, 64 * GROUP), (vis, vraw, 4 * GROUP)))
    ]
    for copy in mine:
        copy.start()
    barrier = pltpu.get_barrier_semaphore()
    for peer in [base + to[o] for o in range(1, GROUP)] + [xpeer] + zpeer[1:]:
        pl.semaphore_signal(barrier, inc=1, device_id=peer, device_id_type=LOGICAL)

    lane = lax.broadcasted_iota(jnp.int32, (8, 128), 1) // OWN
    ids = pairs[...].astype(f32)
    ids = jnp.concatenate(
        [ids[side : side + 1, 128 * t : 128 * t + 128] for side in range(2) for t in range(4)], axis=0
    )
    mine[0].wait()
    mine[1].wait()
    jwide[:, 0:OWN] = jraw[...]
    dwide[:, 0:OWN] = draw[...]

    @pl.loop(0, GROUP)
    def _(f):
        for h in range(2):
            for src, dst in ((jwide, jmsg), (dwide, dual)):
                out = None
                for a in range(4):
                    part = src[pl.ds(f + (a * DIRS + 8 * h) * GROUP, 8, stride=GROUP), :]
                    part = pltpu.roll(part, OWN * a, 1) if a else part
                    out = part if out is None else jnp.where(lane == a, part, out)
                dst[f, 8 * h : 8 * h + 8] = out
        jmsg[f, 16:24] = ids

    def basis(f, b):
        return table[(base + f) * NPOLY + b]

    def fit(it, target):
        total = [jnp.zeros((DIRS, 128), f32) for _ in range(NPOLY)]
        for f in range(GROUP):
            value = target(f)
            for b in range(NPOLY):
                total[b] += basis(f, b) * value
        for b in range(NPOLY):
            coef[2 * it, b] = total[b]

    fit(0, lambda f: jmsg[f, 0:16] + dual[f])
    for copy in mine[2:]:
        copy.wait()

    @pl.loop(0, GROUP)
    def _(f):
        for t in range(ROWS // 128):
            at = slice(128 * t, 128 * t + 128)
            for k in range(0, 64, 8):
                cown[f, k : k + 8, at] = raw[pl.ds(f + (64 * t + k) * GROUP, 8, stride=GROUP)]
            cown[f, 64:68, at] = vraw[pl.ds(f + 4 * t * GROUP, 4, stride=GROUP)]

    C[me] = cown[me]
    J[me] = jmsg[me]
    pl.semaphore_wait(barrier, 23)

    def remote(kind, o, src, dst):
        return pltpu.make_async_remote_copy(
            src_ref=src, dst_ref=dst, send_sem=ssem.at[kind, o], recv_sem=rsem.at[kind, o],
            device_id=base + to[o] if isinstance(o, int) else base, device_id_type=LOGICAL,
        )

    def jones_to(o):
        return remote(0, o, jmsg.at[to[o]], J.at[me])

    def coh_to(o):
        return remote(1, o, cown.at[to[o]], C.at[me])

    def coh_from(o):
        return remote(1, o, cown.at[0], C.at[0])

    def u_to(o):
        return remote(2, o, usend.at[to[o]], U.at[me])

    def j1_to(o):
        return remote(3, o, j1send.at[to[o]], J1.at[me])

    def s2_to(o):
        return remote(4, o, s2send.at[to[o]], S2.at[me])

    def x_copy(it):
        return pltpu.make_async_remote_copy(
            src_ref=coef.at[2 * it], dst_ref=xbuf.at[it], send_sem=cs.at[it, 0], recv_sem=cr.at[it, 0],
            device_id=xpeer, device_id_type=LOGICAL,
        )

    def z_copy(it, o):
        return pltpu.make_async_remote_copy(
            src_ref=coef.at[2 * it + 1], dst_ref=zbuf.at[it, o], send_sem=cs.at[it, o], recv_sem=cr.at[it, o],
            device_id=zpeer[o], device_id_type=LOGICAL,
        )

    def fit_x(it):
        x_copy(it).wait_recv()
        coef[2 * it + 1] = coef[2 * it] + xbuf[it]
        for o in ZORDER:
            z_copy(it, o).start()

    def fit_z(it):
        for o in ZORDER:
            z_copy(it, o).wait_recv()
        total = [coef[2 * it + 1, b] for b in range(NPOLY)]
        for o in range(1, 8):
            for b in range(NPOLY):
                total[b] += zbuf[it, o, b]
        return lambda f: sum(basis(f, b) * total[b] for b in range(NPOLY))

    x_copy(0).start()
    for o in range(1, GROUP):
        jones_to(o).start()
    for o in range(1, 8):
        coh_to(o).start()
    fit_x(0)
    for o in range(8, GROUP):
        coh_to(o).start()
    acc[...] = jnp.zeros_like(acc)
    for o in range(1, GROUP):
        jones_to(o).wait_recv()

    for q in range(4):
        for a, block in enumerate(regroup([J[4 * q + i, 0:16] for i in range(4)])):
            g_ref[16 * a : 16 * a + 16, 128 * q : 128 * q + 128] = block
    set_table(g_ref, gcat)

    @pl.loop(0, GROUP)
    def _(b):
        build_onehot(J, oh, b)

    @pl.loop(0, GROUP)
    def _(o):
        b = fro(o)

        @pl.when(o == 7)
        def _():
            fitted = fit_z(0)
            for f in range(GROUP):
                u = fitted(f) - dual[f]
                u_own[f] = u
                usend[f] = u
            U[me] = u_own[me]
            for o in range(1, GROUP):
                u_to(o).start()

        @pl.when(o > 0)
        def _():
            coh_from(o).wait_recv()

        x0[...] = jnp.dot(gcat[...], oh[b], preferred_element_type=f32)
        row_terms(C, J, x0, s0, b)
        acc[...] += lax.dot_general(
            s0[...], oh[b], (((1,), (1,)), ((), ())), preferred_element_type=f32
        )

    def sums(comp, pol, q):
        o, at = (q // 2) * 192 + comp * 32 + pol * 16, slice((q % 2) * 128, (q % 2) * 128 + 128)
        return acc[o : o + 16, at] + acc[o + 96 : o + 112, at]

    row = lax.broadcasted_iota(jnp.int32, (DIRS, 128), 0)
    weight = jnp.zeros((DIRS, 128), f32)
    for k in range(DIRS):
        weight = jnp.where(row == k, pen[k], weight)

    for o in range(1, GROUP):
        u_to(o).wait_recv()

    for q in range(4):
        u = regroup([U[4 * q + i] for i in range(4)])
        wide = [sums(2, pol, q) + weight for pol in range(2)]
        new = []
        for a in range(4):
            gain = g_ref[16 * a : 16 * a + 16, 128 * q : 128 * q + 128]
            gain = gain + (sums(a // 2, a % 2, q) + weight * (u[a] - gain)) / wide[a % 2]
            g_ref[16 * a : 16 * a + 16, 128 * q : 128 * q + 128] = gain
            new.append(gain)
        for i, slab in enumerate(regroup(new)):
            j1send[4 * q + i] = slab
    for o in range(1, GROUP):
        j1_to(o).start()
    J1[me] = j1send[me]
    set_table(g_ref, gcat)
    acc[...] = jnp.zeros_like(acc)

    @pl.loop(0, 4)
    def _(i):
        @pl.when(i == 2)
        def _():
            for o in range(1, GROUP):
                j1_to(o).wait_recv()
            fit(1, lambda f: 2.0 * J1[f] - u_own[f])
            x_copy(1).start()

        @pl.when(i == 3)
        def _():
            fit_x(1)

        for k, xs in enumerate((x0, x1, x2, x3)):
            xs[...] = jnp.dot(gcat[...], oh[4 * i + k], preferred_element_type=f32)
        for k, (xs, ss) in enumerate(((x0, s0), (x1, s1), (x2, s2), (x3, s3))):
            row_terms(C, J, xs, ss, 4 * i + k)
        total = acc[...]
        for k, ss in enumerate((s0, s1, s2, s3)):
            total += lax.dot_general(
                ss[...], oh[4 * i + k], (((1,), (1,)), ((), ())), preferred_element_type=f32
            )
        acc[...] = total

    for q in range(4):
        grads = regroup([sums(a // 2, a % 2, q) for a in range(4)])
        wides = [sums(2, pol, q) for pol in range(2)]
        wides = regroup([wides[a % 2][8 * (a // 2) : 8 * (a // 2) + 8] for a in range(4)])
        for i in range(4):
            s2send[4 * q + i, 0:16] = grads[i]
            s2send[4 * q + i, 16:24] = wides[i]
    for o in range(1, GROUP):
        s2_to(o).start()
    S2[me] = s2send[me]

    fitted = fit_z(1)
    for f in range(GROUP):
        u_own[f] = fitted(f) - (J1[f] - u_own[f])
    for o in range(1, GROUP):
        s2_to(o).wait_recv()

    low = lane < 2

    @pl.loop(0, GROUP)
    def _(f):
        packed = S2[f, 16:24]
        turned = pltpu.roll(packed, 64, 1)
        for h, wide in enumerate((jnp.where(low, packed, turned), jnp.where(low, turned, packed))):
            at = slice(8 * h, 8 * h + 8)
            gain, u, pk = J1[f, at], u_own[f, at], weight[at]
            gain = gain + (S2[f, at] + pk * (u - gain)) / (wide + pk)
            for value, dst in ((gain, jones_out), (gain - u, duals_out)):
                for a in range(4):
                    part = pltpu.roll(value, 128 - OWN * a, 1) if a else value
                    dst[pl.ds(f + (a * DIRS + 8 * h) * GROUP, 8, stride=GROUP), :] = part

    for o in range(1, GROUP):
        for copy in (jones_to, coh_to, u_to, j1_to, s2_to):
            copy(o).wait_send()
    for it in range(2):
        x_copy(it).wait_send()
        for o in ZORDER:
            z_copy(it, o).wait_send()


def body(visibility, coherency, station_pairs, jones_gains, scaled_duals, penalty):
    state = jones_gains.shape
    wide = jax.ShapeDtypeStruct((64 * GROUP, 128), f32)
    slab = (GROUP, DIRS, 128)
    msg = (GROUP, DIRS + 8, 128)
    hbm, vmem, smem = [
        pl.BlockSpec(memory_space=space) for space in (pltpu.HBM, pltpu.VMEM, pltpu.SMEM)
    ]
    outs = pl.pallas_call(
        kernel,
        out_shape=(wide, wide),
        in_specs=[hbm, hbm, vmem, hbm, hbm, smem, smem],
        out_specs=(vmem, vmem),
        scratch_shapes=[
            pltpu.VMEM((4 * 64 * GROUP, 128), f32),
            pltpu.VMEM((4 * 4 * GROUP, 128), f32),
            pltpu.VMEM((64 * GROUP, OWN), f32),
            pltpu.VMEM((64 * GROUP, OWN), f32),
            pltpu.VMEM((64 * GROUP, 128), f32),
            pltpu.VMEM((64 * GROUP, 128), f32),
            pltpu.VMEM((GROUP, 68, ROWS), f32),
            pltpu.VMEM(msg, f32),
            pltpu.VMEM(slab, f32),
            pltpu.VMEM((GROUP, 68, ROWS), f32),
            pltpu.VMEM(msg, f32),
            pltpu.VMEM(slab, f32),
            pltpu.VMEM(slab, f32),
            pltpu.VMEM(msg, f32),
            pltpu.VMEM((64, STATIONS), f32),
            pltpu.VMEM(slab, f32),
            pltpu.VMEM(slab, f32),
            pltpu.VMEM(slab, f32),
            pltpu.VMEM(msg, f32),
            pltpu.VMEM((4, NPOLY, DIRS, 128), f32),
            pltpu.VMEM((2, NPOLY, DIRS, 128), f32),
            pltpu.VMEM((2, 8, NPOLY, DIRS, 128), f32),
            pltpu.VMEM((GROUP, HALF, 2 * ROWS), bf16),
            pltpu.VMEM((256, HALF), bf16),
            pltpu.VMEM((384, HALF), f32),
        ]
        + [pltpu.VMEM((256, 2 * ROWS), f32)] * 4
        + [pltpu.VMEM((384, 2 * ROWS), bf16)] * 4
        + [
            pltpu.SemaphoreType.DMA((5, GROUP)),
            pltpu.SemaphoreType.DMA((5, GROUP)),
            pltpu.SemaphoreType.DMA((3, 4)),
            pltpu.SemaphoreType.DMA((2, 8)),
            pltpu.SemaphoreType.DMA((2, 8)),
        ],
        compiler_params=pltpu.CompilerParams(
            collective_id=0, has_side_effects=True, vmem_limit_bytes=56 * 2**20
        ),
    )(
        coherency.reshape(64 * GROUP, ROWS),
        visibility.reshape(4 * GROUP, ROWS),
        station_pairs,
        jones_gains.reshape(64 * GROUP, OWN),
        scaled_duals.reshape(64 * GROUP, OWN),
        penalty,
        jnp.asarray(cosine_table().reshape(-1)),
    )
    return tuple(out[:, :OWN].reshape(state) for out in outs)


def solution(mesh):
    state = P(None, None, None, "chan", "bl")
    return jax.shard_map(
        body,
        mesh=mesh,
        in_specs=(P(None, None, "chan", "bl"), state, P(None, "bl"), state, state, P()),
        out_specs=(state, state),
        check_vma=False,
    )
```

time: 94.2 us -> 73.7 us (0.78)
  Pallas kernels: 87 us -> 69.1 us
  local copies, waits for them, and re-layouts: 6.41 us -> 3.74 us
    pallas_call x1, Pallas kernels: 87 us -> 69.1 us  [body(): pl.pallas_call(kernel, out_shape=(wide, wide), in_specs=[hbm, hbm, vmem,...]
    transpose x3 -> x0, local copies, waits for them, and re-layouts: 4.63 us -> none  [the longest x2 3.05 us: pack(): return jnp.transpose(state, (3, 2, 0, 1, 4)).reshape(GROUP, DIRS, 128)]
    unnamed x10 -> x2, local copies, waits for them, and re-layouts: 0.02 us -> 3.74 us
    reshape x4 -> x0, local copies, waits for them, and re-layouts: 1.76 us -> none  [the longest x2 0.89 us: pack(): return jnp.transpose(state, (3, 2, 0, 1, 4)).reshape(GROUP, DIRS, 128)]
where the time goes in v2:
time: 73.7 us; the launch traced here: 73.4 us
  Pallas kernels  69.1 us (94%)
  local copies, waits for them, and re-layouts  3.74 us (5%)
    pallas_call x1, Pallas kernels, body(): pl.pallas_call(kernel, out_shape=(wide, wide), in_specs=[hbm, hbm, vmem,...  69.1 us
    unnamed x2, local copies, waits for them, and re-layouts  3.74 us

profile of v2, /device:TPU:1, one launch (start us, length us, event | category | flops | bytes accessed | tf_op | source)
XLA Modules:
  0.0 73.4 jit_solution(10657063570944373746)
XLA Ops:
  0.6 69.1 %shard_map.86 = (f32[1024,128]{1,0:T(8,128)}, f32[1024,128]{1,0:T(8,128)}) custom-call(f32[1024,512]{1,0:T(8,128)} %bitcast.8, f32[64,512]{1,0:T(8,128)} %bitcast.13, s32[2,512]{1,0:T(2,128)} %pairs.1, f32[1024,32]{1,0:T(8,128)} %bitcast.11, f32[1024,32]{1,0:T(8,128)} %bitcast.12, f32[16]{0:T(128)} %pen.1, f32[768]{0:T(1024)} %constant.2.clone.table), custom_call_target="tpu_custom_call" | custom-call | tf_op jit(solution)/shard_map/pallas_call | solution.py:396
  69.7 1.9 %copy.11 = f32[2,2,16,16,32]{4,3,2,1,0:T(8,128)} copy(f32[2,2,16,16,32]{4,3,2,1,0:T(8,128)} %bitcast.10) | data formatting | bytes 262144
  71.6 1.9 %copy.12 = f32[2,2,16,16,32]{4,3,2,1,0:T(8,128)} copy(f32[2,2,16,16,32]{4,3,2,1,0:T(8,128)} %bitcast.9) | data formatting | bytes 262144

commit v3 on v2

--- a/solution.py
+++ b/solution.py
@@ -19,6 +19,7 @@
 HALF = 256
 LOGICAL = pl.DeviceIdType.LOGICAL
 ZORDER = (1, 7, 2, 6, 3, 5, 4)
+FIRST, AMID, PAIR, USEND = 3, 8, 2, 4
 f32, bf16 = jnp.float32, jnp.bfloat16
 
 
@@ -78,14 +79,15 @@
                 return jnp.where(upper[side], h1, h0) + jnp.where(upper[side], l1, l0)
 
             pr, pi, qr, qi = gain(0, 0), gain(0, 1), gain(1, 0), gain(1, 1)
-            cr = c_ref[b, 16 * pol : 16 * pol + 16, l : l + n]
-            ci = c_ref[b, 32 + 16 * pol : 48 + 16 * pol, l : l + n]
+            cr = c_ref[b, l // 2 + 16 * pol : l // 2 + 16 * pol + 16, :]
+            ci = c_ref[b, l // 2 + 32 + 16 * pol : l // 2 + 48 + 16 * pol, :]
             dr = pr * cr - pi * ci
             di = pr * ci + pi * cr
             mr = dr * qr + di * qi
             mi = di * qr - dr * qi
-            rr = c_ref[b, 64 + pol : 65 + pol, l : l + n] - jnp.sum(mr, axis=0, keepdims=True)
-            ri = c_ref[b, 66 + pol : 67 + pol, l : l + n] - jnp.sum(mi, axis=0, keepdims=True)
+            v = 256 + l // 32 + pol
+            rr = c_ref[b, v : v + 1, :] - jnp.sum(mr, axis=0, keepdims=True)
+            ri = c_ref[b, v + 2 : v + 3, :] - jnp.sum(mi, axis=0, keepdims=True)
             sr = cr * qr + ci * qi
             si = ci * qr - cr * qi
             first = (rr * sr + ri * si, ri * sr - rr * si, sr * sr + si * si)
@@ -108,6 +110,13 @@
     return jnp.where(v >= n, v - n, v)
 
 
+def turn(p):
+    return (GROUP - p) % GROUP
+
+
+ORDER = [turn(p) for p in range(GROUP)]
+
+
 def kernel(
     coh, vis, pairs, jones, duals, pen, table,
     jones_out, duals_out,
@@ -149,6 +158,83 @@
     ids = jnp.concatenate(
         [ids[side : side + 1, 128 * t : 128 * t + 128] for side in range(2) for t in range(4)], axis=0
     )
+    def relay(f):
+        for t in range(ROWS // 128):
+            for k in range(64 * t, 64 * t + 64, 8):
+                cown[f, k : k + 8] = raw[pl.ds(f + k * GROUP, 8, stride=GROUP)]
+            cown[f, 256 + 4 * t : 260 + 4 * t] = vraw[pl.ds(f + 4 * t * GROUP, 4, stride=GROUP)]
+
+    def basis(f, b):
+        return table[(base + f) * NPOLY + b]
+
+    def fit(it, target):
+        total = [jnp.zeros((DIRS, 128), f32) for _ in range(NPOLY)]
+        for f in range(GROUP):
+            value = target(f)
+            for b in range(NPOLY):
+                total[b] += basis(f, b) * value
+        for b in range(NPOLY):
+            coef[2 * it, b] = total[b]
+
+    def remote(kind, o, src, dst):
+        return pltpu.make_async_remote_copy(
+            src_ref=src, dst_ref=dst, send_sem=ssem.at[kind, o], recv_sem=rsem.at[kind, o],
+            device_id=base + to[o] if isinstance(o, int) else base, device_id_type=LOGICAL,
+        )
+
+    def jones_to(o):
+        return remote(0, o, jmsg.at[to[o]], J.at[me])
+
+    def coh_to(o):
+        return remote(1, o, cown.at[to[o]], C.at[me])
+
+    def coh_from(o):
+        return remote(1, o, cown.at[0], C.at[0])
+
+    def u_to(o):
+        return remote(2, o, usend.at[to[o]], U.at[me])
+
+    def j1_to(o):
+        return remote(3, o, j1send.at[to[o]], J1.at[me])
+
+    def s2_to(o):
+        return remote(4, o, s2send.at[to[o]], S2.at[me])
+
+    def x_copy(it):
+        return pltpu.make_async_remote_copy(
+            src_ref=coef.at[2 * it], dst_ref=xbuf.at[it], send_sem=cs.at[it, 0], recv_sem=cr.at[it, 0],
+            device_id=xpeer, device_id_type=LOGICAL,
+        )
+
+    def z_copy(it, o):
+        return pltpu.make_async_remote_copy(
+            src_ref=coef.at[2 * it + 1], dst_ref=zbuf.at[it, o], send_sem=cs.at[it, o], recv_sem=cr.at[it, o],
+            device_id=zpeer[o], device_id_type=LOGICAL,
+        )
+
+    def fit_x(it):
+        x_copy(it).wait_recv()
+        coef[2 * it + 1] = coef[2 * it] + xbuf[it]
+        for o in ZORDER:
+            z_copy(it, o).start()
+
+    def fit_z(it):
+        for o in ZORDER:
+            z_copy(it, o).wait_recv()
+        total = [coef[2 * it + 1, b] for b in range(NPOLY)]
+        for o in range(1, 8):
+            for b in range(NPOLY):
+                total[b] += zbuf[it, o, b]
+        return lambda f: sum(basis(f, b) * total[b] for b in range(NPOLY))
+
+    for copy in mine[2:]:
+        copy.wait()
+    for p in range(1, FIRST):
+        relay(to[ORDER[p]])
+    pl.semaphore_wait(barrier, 23)
+    for p in range(1, FIRST):
+        coh_to(ORDER[p]).start()
+
     mine[0].wait()
     mine[1].wait()
     jwide[:, 0:OWN] = jraw[...]
@@ -166,94 +252,22 @@
                 dst[f, 8 * h : 8 * h + 8] = out
         jmsg[f, 16:24] = ids
 
-    def basis(f, b):
-        return table[(base + f) * NPOLY + b]
-
-    def fit(it, target):
-        total = [jnp.zeros((DIRS, 128), f32) for _ in range(NPOLY)]
-        for f in range(GROUP):
-            value = target(f)
-            for b in range(NPOLY):
-                total[b] += basis(f, b) * value
-        for b in range(NPOLY):
-            coef[2 * it, b] = total[b]
-
     fit(0, lambda f: jmsg[f, 0:16] + dual[f])
-    for copy in mine[2:]:
-        copy.wait()
-
-    @pl.loop(0, GROUP)
-    def _(f):
-        for t in range(ROWS // 128):
-            at = slice(128 * t, 128 * t + 128)
-            for k in range(0, 64, 8):
-                cown[f, k : k + 8, at] = raw[pl.ds(f + (64 * t + k) * GROUP, 8, stride=GROUP)]
-            cown[f, 64:68, at] = vraw[pl.ds(f + 4 * t * GROUP, 4, stride=GROUP)]
-
+    x_copy(0).start()
+    for o in range(1, GROUP):
+        jones_to(o).start()
+    for p in range(FIRST, AMID):
+        relay(to[ORDER[p]])
+        coh_to(ORDER[p]).start()
+    J[me] = jmsg[me]
+    for p in range(AMID, GROUP):
+        relay(to[ORDER[p]])
+    relay(me)
     C[me] = cown[me]
-    J[me] = jmsg[me]
-    pl.semaphore_wait(barrier, 23)
-
-    def remote(kind, o, src, dst):
-        return pltpu.make_async_remote_copy(
-            src_ref=src, dst_ref=dst, send_sem=ssem.at[kind, o], recv_sem=rsem.at[kind, o],
-            device_id=base + to[o] if isinstance(o, int) else base, device_id_type=LOGICAL,
-        )
-
-    def jones_to(o):
-        return remote(0, o, jmsg.at[to[o]], J.at[me])
-
-    def coh_to(o):
-        return remote(1, o, cown.at[to[o]], C.at[me])
-
-    def coh_from(o):
-        return remote(1, o, cown.at[0], C.at[0])
-
-    def u_to(o):
-        return remote(2, o, usend.at[to[o]], U.at[me])
-
-    def j1_to(o):
-        return remote(3, o, j1send.at[to[o]], J1.at[me])
-
-    def s2_to(o):
-        return remote(4, o, s2send.at[to[o]], S2.at[me])
-
-    def x_copy(it):
-        return pltpu.make_async_remote_copy(
-            src_ref=coef.at[2 * it], dst_ref=xbuf.at[it], send_sem=cs.at[it, 0], recv_sem=cr.at[it, 0],
-            device_id=xpeer, device_id_type=LOGICAL,
-        )
-
-    def z_copy(it, o):
-        return pltpu.make_async_remote_copy(
-            src_ref=coef.at[2 * it + 1], dst_ref=zbuf.at[it, o], send_sem=cs.at[it, o], recv_sem=cr.at[it, o],
-            device_id=zpeer[o], device_id_type=LOGICAL,
-        )
-
-    def fit_x(it):
-        x_copy(it).wait_recv()
-        coef[2 * it + 1] = coef[2 * it] + xbuf[it]
-        for o in ZORDER:
-            z_copy(it, o).start()
-
-    def fit_z(it):
-        for o in ZORDER:
-            z_copy(it, o).wait_recv()
-        total = [coef[2 * it + 1, b] for b in range(NPOLY)]
-        for o in range(1, 8):
-            for b in range(NPOLY):
-                total[b] += zbuf[it, o, b]
-        return lambda f: sum(basis(f, b) * total[b] for b in range(NPOLY))
-
-    x_copy(0).start()
-    for o in range(1, GROUP):
-        jones_to(o).start()
-    for o in range(1, 8):
-        coh_to(o).start()
+    acc[...] = jnp.zeros_like(acc)
     fit_x(0)
-    for o in range(8, GROUP):
-        coh_to(o).start()
-    acc[...] = jnp.zeros_like(acc)
+    for p in range(AMID, GROUP):
+        coh_to(ORDER[p]).start()
     for o in range(1, GROUP):
         jones_to(o).wait_recv()
 
@@ -266,11 +280,22 @@
     def _(b):
         build_onehot(J, oh, b)
 
-    @pl.loop(0, GROUP)
-    def _(o):
-        b = fro(o)
-
-        @pl.when(o == 7)
+    def rows(blocks):
+        work = list(zip(blocks, (x0, x1, x2, x3), (s0, s1, s2, s3)))
+        for b, xs, ss in work:
+            xs[...] = jnp.dot(gcat[...], oh[b], preferred_element_type=f32)
+        for b, xs, ss in work:
+            row_terms(C, J, xs, ss, b)
+        total = acc[...]
+        for b, xs, ss in work:
+            total += lax.dot_general(
+                ss[...], oh[b], (((1,), (1,)), ((), ())), preferred_element_type=f32
+            )
+        acc[...] = total
+
+    @pl.loop(0, GROUP // PAIR)
+    def _(i):
+        @pl.when(i == USEND)
         def _():
             fitted = fit_z(0)
             for f in range(GROUP):
@@ -281,15 +306,20 @@
             for o in range(1, GROUP):
                 u_to(o).start()
 
-        @pl.when(o > 0)
-        def _():
-            coh_from(o).wait_recv()
-
-        x0[...] = jnp.dot(gcat[...], oh[b], preferred_element_type=f32)
-        row_terms(C, J, x0, s0, b)
-        acc[...] += lax.dot_general(
-            s0[...], oh[b], (((1,), (1,)), ((), ())), preferred_element_type=f32
-        )
+        blocks = []
+        for k in range(PAIR):
+            p = PAIR * i + k
+            o = turn(p)
+            blocks.append(fro(o))
+            if k:
+                coh_from(o).wait_recv()
+            else:
+
+                @pl.when(p > 0)
+                def _():
+                    coh_from(o).wait_recv()
+
+        rows(blocks)
 
     def sums(comp, pol, q):
         o, at = (q // 2) * 192 + comp * 32 + pol * 16, slice((q % 2) * 128, (q % 2) * 128 + 128)
@@ -333,16 +363,7 @@
         def _():
             fit_x(1)
 
-        for k, xs in enumerate((x0, x1, x2, x3)):
-            xs[...] = jnp.dot(gcat[...], oh[4 * i + k], preferred_element_type=f32)
-        for k, (xs, ss) in enumerate(((x0, s0), (x1, s1), (x2, s2), (x3, s3))):
-            row_terms(C, J, xs, ss, 4 * i + k)
-        total = acc[...]
-        for k, ss in enumerate((s0, s1, s2, s3)):
-            total += lax.dot_general(
-                ss[...], oh[4 * i + k], (((1,), (1,)), ((), ())), preferred_element_type=f32
-            )
-        acc[...] = total
+        rows([4 * i + k for k in range(4)])
 
     for q in range(4):
         grads = regroup([sums(a // 2, a % 2, q) for a in range(4)])
@@ -371,10 +392,8 @@
             at = slice(8 * h, 8 * h + 8)
             gain, u, pk = J1[f, at], u_own[f, at], weight[at]
             gain = gain + (S2[f, at] + pk * (u - gain)) / (wide + pk)
-            for value, dst in ((gain, jones_out), (gain - u, duals_out)):
-                for a in range(4):
-                    part = pltpu.roll(value, 128 - OWN * a, 1) if a else value
-                    dst[pl.ds(f + (a * DIRS + 8 * h) * GROUP, 8, stride=GROUP), :] = part
+            jones_out[f, at] = gain
+            duals_out[f, at] = gain - u
 
     for o in range(1, GROUP):
         for copy in (jones_to, coh_to, u_to, j1_to, s2_to):
@@ -386,16 +405,15 @@
 
 
 def body(visibility, coherency, station_pairs, jones_gains, scaled_duals, penalty):
-    state = jones_gains.shape
-    wide = jax.ShapeDtypeStruct((64 * GROUP, 128), f32)
     slab = (GROUP, DIRS, 128)
+    packed = jax.ShapeDtypeStruct(slab, f32)
     msg = (GROUP, DIRS + 8, 128)
     hbm, vmem, smem = [
         pl.BlockSpec(memory_space=space) for space in (pltpu.HBM, pltpu.VMEM, pltpu.SMEM)
     ]
-    outs = pl.pallas_call(
+    packed = pl.pallas_call(
         kernel,
-        out_shape=(wide, wide),
+        out_shape=(packed, packed),
         in_specs=[hbm, hbm, vmem, hbm, hbm, smem, smem],
         out_specs=(vmem, vmem),
         scratch_shapes=[
@@ -405,10 +423,10 @@
             pltpu.VMEM((64 * GROUP, OWN), f32),
             pltpu.VMEM((64 * GROUP, 128), f32),
             pltpu.VMEM((64 * GROUP, 128), f32),
-            pltpu.VMEM((GROUP, 68, ROWS), f32),
+            pltpu.VMEM((GROUP, 272, 128), f32),
             pltpu.VMEM(msg, f32),
             pltpu.VMEM(slab, f32),
-            pltpu.VMEM((GROUP, 68, ROWS), f32),
+            pltpu.VMEM((GROUP, 272, 128), f32),
             pltpu.VMEM(msg, f32),
             pltpu.VMEM(slab, f32),
             pltpu.VMEM(slab, f32),
@@ -446,7 +464,8 @@
         penalty,
         jnp.asarray(cosine_table().reshape(-1)),
     )
-    return tuple(out[:, :OWN].reshape(state) for out in outs)
+    outs = [out.reshape(GROUP, DIRS, 2, 2, OWN) for out in packed]
+    return tuple(jnp.transpose(out, (2, 3, 1, 0, 4)) for out in outs)
 
 
 def solution(mesh):

time: 73.7 us -> 71.5 us (0.970)
  Pallas kernels: 69.1 us -> 66.4 us
    unnamed x2 -> x0, local copies, waits for them, and re-layouts: 3.74 us -> none
    reshape x0 -> x2, local copies, waits for them, and re-layouts: none -> 2.68 us  [body(): outs = [out.reshape(GROUP, DIRS, 2, 2, OWN) for out in packed]]
    pallas_call x1, Pallas kernels: 69.1 us -> 66.4 us  [body(): pl.pallas_call(kernel, out_shape=(packed, packed), in_specs=[hbm, hbm, vm...]
    transpose x0 -> x1, local copies, waits for them, and re-layouts: none -> 1.58 us  [body(): return tuple((jnp.transpose(out, (2, 3, 1, 0, 4)) for out in outs))]
where the time goes in v3:
time: 71.5 us; the launch traced here: 71.3 us
  Pallas kernels  66.4 us (93%)
  local copies, waits for them, and re-layouts  4.26 us (6%)
    pallas_call x1, Pallas kernels, body(): pl.pallas_call(kernel, out_shape=(packed, packed), in_specs=[hbm, hbm, vm...  66.4 us
    reshape x2, local copies, waits for them, and re-layouts, body(): outs = [out.reshape(GROUP, DIRS, 2, 2, OWN) for out in packed]  2.68 us
    transpose x1, local copies, waits for them, and re-layouts, body(): return tuple((jnp.transpose(out, (2, 3, 1, 0, 4)) for out in outs))  1.58 us

profile of v3, /device:TPU:1, one launch (start us, length us, event | category | flops | bytes accessed | tf_op | source)
XLA Modules:
  0.0 71.3 jit_solution(8789634115409016669)
XLA Ops:
  0.6 66.4 %shard_map.86 = (f32[16,16,128]{2,1,0:T(8,128)}, f32[16,16,128]{2,1,0:T(8,128)}) custom-call(f32[1024,512]{1,0:T(8,128)} %bitcast.8, f32[64,512]{1,0:T(8,128)} %bitcast.11, s32[2,512]{1,0:T(2,128)} %pairs.1, f32[1024,32]{1,0:T(8,128)} %bitcast.9, f32[1024,32]{1,0:T(8,128)} %bitcast.10, f32[16]{0:T(128)} %pen.1, f32[768]{0:T(1024)} %constant.2.clone.table), custom_call_target="tpu_custom_call" | custom-call | tf_op jit(solution)/shard_map/pallas_call | solution.py:414
  67.1 1.3 %reshape.26 = f32[16,16,2,2,32]{4,3,2,1,0:T(2,128)S(1)} reshape(f32[16,16,128]{2,1,0:T(8,128)} %get-tuple-element.4) | data formatting | bytes 262144 | tf_op jit(solution)/shard_map/reshape | solution.py:467
  68.4 1.3 %reshape.27 = f32[16,16,2,2,32]{4,3,2,1,0:T(2,128)S(1)} reshape(f32[16,16,128]{2,1,0:T(8,128)} %get-tuple-element.5) | data formatting | bytes 262144 | tf_op jit(solution)/shard_map/reshape | solution.py:467
  69.8 1.6 %copy_bitcast_fusion = (f32[2,2,16,16,32]{4,3,2,1,0:T(8,128)}, f32[2,2,16,16,32]{4,3,2,1,0:T(8,128)}) fusion(f32[16,16,2,2,32]{4,3,2,1,0:T(2,128)S(1)} %reshape.27, f32[16,16,2,2,32]{4,3,2,1,0:T(2,128)S(1)} %reshape.26), kind=kLoop, calls=%fused_computation | loop fusion | bytes 524288 | tf_op jit(solution)/shard_map/transpose | solution.py:468

commit v4 on v3

--- a/solution.py
+++ b/solution.py
@@ -19,7 +19,7 @@
 HALF = 256
 LOGICAL = pl.DeviceIdType.LOGICAL
 ZORDER = (1, 7, 2, 6, 3, 5, 4)
-FIRST, AMID, PAIR, USEND = 3, 8, 2, 4
+FIRST, AMID, PAIR, USEND = 3, 8, 4, 2
 f32, bf16 = jnp.float32, jnp.bfloat16
 
 

time: 71.5 us -> 71 us (level)
  no operation moved by 1% of the time
where the time goes in v4:
time: 71 us; the launch traced here: 70.9 us
  Pallas kernels  66 us (93%)
  local copies, waits for them, and re-layouts  4.26 us (6%)
    pallas_call x1, Pallas kernels, body(): pl.pallas_call(kernel, out_shape=(packed, packed), in_specs=[hbm, hbm, vm...  66 us
    reshape x2, local copies, waits for them, and re-layouts, body(): outs = [out.reshape(GROUP, DIRS, 2, 2, OWN) for out in packed]  2.68 us
    transpose x1, local copies, waits for them, and re-layouts, body(): return tuple((jnp.transpose(out, (2, 3, 1, 0, 4)) for out in outs))  1.58 us

profile of v4, /device:TPU:1, one launch (start us, length us, event | category | flops | bytes accessed | tf_op | source)
XLA Modules:
  0.0 70.9 jit_solution(16724664137530956997)
XLA Ops:
  0.6 66.0 %shard_map.86 = (f32[16,16,128]{2,1,0:T(8,128)}, f32[16,16,128]{2,1,0:T(8,128)}) custom-call(f32[1024,512]{1,0:T(8,128)} %bitcast.8, f32[64,512]{1,0:T(8,128)} %bitcast.11, s32[2,512]{1,0:T(2,128)} %pairs.1, f32[1024,32]{1,0:T(8,128)} %bitcast.9, f32[1024,32]{1,0:T(8,128)} %bitcast.10, f32[16]{0:T(128)} %pen.1, f32[768]{0:T(1024)} %constant.2.clone.table), custom_call_target="tpu_custom_call" | custom-call | tf_op jit(solution)/shard_map/pallas_call | solution.py:414
  66.6 1.3 %reshape.26 = f32[16,16,2,2,32]{4,3,2,1,0:T(2,128)S(1)} reshape(f32[16,16,128]{2,1,0:T(8,128)} %get-tuple-element.4) | data formatting | bytes 262144 | tf_op jit(solution)/shard_map/reshape | solution.py:467
  68.0 1.3 %reshape.27 = f32[16,16,2,2,32]{4,3,2,1,0:T(2,128)S(1)} reshape(f32[16,16,128]{2,1,0:T(8,128)} %get-tuple-element.5) | data formatting | bytes 262144 | tf_op jit(solution)/shard_map/reshape | solution.py:467
  69.3 1.6 %copy_bitcast_fusion = (f32[2,2,16,16,32]{4,3,2,1,0:T(8,128)}, f32[2,2,16,16,32]{4,3,2,1,0:T(8,128)}) fusion(f32[16,16,2,2,32]{4,3,2,1,0:T(2,128)S(1)} %reshape.27, f32[16,16,2,2,32]{4,3,2,1,0:T(2,128)S(1)} %reshape.26), kind=kLoop, calls=%fused_computation | loop fusion | bytes 524288 | tf_op jit(solution)/shard_map/transpose | solution.py:468
